TPU v7x, 256 devices: a whole 4x4x8 slice. The times are simulated.
256 devices in a mesh: ctx: 64 (over z, x, core), head: 4 (over y).
Axes of the slice: x: 4, y: 4, z: 8, core: 2. Of those that a mesh axis runs over, the one named last changes fastest.
Arguments:
- queries: bfloat16 [8192, 4096], P('ctx', 'head'), may hold values from -40 to 40
- keys: bfloat16 [8192, 4096], P('ctx', 'head'), may hold values from -40 to 40
- values: bfloat16 [8192, 4096], P('ctx', 'head'), may hold values from -50 to 50
- pattern: int32 [64, 8], replicated, may hold values from -1 to 63, as said below
- upstream: bfloat16 [8192, 4096], P('ctx', 'head'), may hold values from -6 to 6
Outputs:
- normed: bfloat16 [8192, 4096], P('ctx', 'head')
- grad_queries: bfloat16 [8192, 4096], P('ctx', 'head')
- grad_keys: bfloat16 [8192, 4096], P('ctx', 'head')
- grad_values: bfloat16 [8192, 4096], P('ctx', 'head')
Inputs may be any that keep to these rules, and one draw needn't show every extreme that they name: `pattern`: entry [i, k] for k < 7 is either i - 2^k or -1, and always -1 where i < 2^k; entry [i, 7] is i.
All inputs are finite; a program needn't handle non-finite values.
Results may differ from a plain program's by a relative error of at most 0.04.
Values may be sent and summed in bfloat16 or wider, within the bound.
A program may use at most 64 MiB of HBM per device.

v0:
```python
import jax
import jax.numpy as jnp
from jax import lax
from jax.sharding import PartitionSpec as P

HD = 128
BLOCK = 128
LEVELS = 7
WIDTH = 4096
NEG_BIG = -1e30
EPSILON = 1e-06


def shifted(block, axis, distance):
    devices = range(lax.axis_size(axis))
    route = [(i - distance, i) for i in devices if i - distance in devices]
    return lax.ppermute(block, axis, route)


def for_sending(x):
    return jax.tree.map(lambda a: a.astype(jnp.bfloat16) if a.dtype == jnp.float32 else a, x)


def route_table(blocks, levels):
    routing = []
    for query_block in range(blocks):
        for level_index in range(levels + 1):
            if level_index == levels:
                routing.append((0, query_block))
            else:
                distance = 2**level_index
                routing.append(
                    (-((query_block - distance) // blocks), (query_block - distance) % blocks)
                )
    return routing


def pair_grads(
    query_tiles, grad_tiles, lse_tiles, delta_tiles, key_tiles, value_tiles, keep_mask, score_scale
):
    scores = (
        jnp.einsum("pqhd,pkhd->phqk", query_tiles, key_tiles, preferred_element_type=jnp.float32)
        * score_scale
    )
    scores = jnp.where(keep_mask[:, None], scores, NEG_BIG)
    weights = jnp.exp(scores - lse_tiles[..., None])
    prob_tiles = weights.astype(jnp.bfloat16)
    grad_probs = jnp.einsum(
        "pqhd,pkhd->phqk", grad_tiles, value_tiles, preferred_element_type=jnp.float32
    )
    dscore = (weights * (grad_probs - delta_tiles[..., None]) * score_scale).astype(jnp.bfloat16)
    return (dscore, prob_tiles)


def key_grads(dscore, prob_tiles, query_tiles, grad_tiles):
    key_part = jnp.einsum(
        "phqk,pqhd->pkhd", dscore, query_tiles, preferred_element_type=jnp.float32
    )
    value_part = jnp.einsum(
        "phqk,pqhd->pkhd", prob_tiles, grad_tiles, preferred_element_type=jnp.float32
    )
    return jnp.stack((key_part, value_part))


def collect(partials, targets, blocks):
    pieces = []
    for key_index in range(blocks):
        summed = jnp.zeros((2,) + partials.shape[2:], jnp.float32)
        for row_index, target in enumerate(targets):
            if target == key_index:
                summed = summed + partials[:, row_index]
        pieces.append(summed)
    return jnp.stack(pieces, axis=1)


def shards(queries, keys, values, pattern, upstream):
    tokens_here = queries.shape[0]
    heads_here = queries.shape[1] // HD
    blocks = tokens_here // BLOCK
    slot_count = LEVELS + 1
    pair_count = blocks * slot_count
    score_scale = HD ** (-0.5)
    ctx_count = lax.axis_size("ctx")
    device_index = lax.axis_index("ctx")
    routing = route_table(blocks, LEVELS)
    offsets = sorted(
        set((route_entry[0] for route_entry in routing if 0 < route_entry[0] < ctx_count))
    )
    tile_shape = (blocks, BLOCK, heads_here, HD)
    query_blocks = queries.reshape(tile_shape)
    own_pairs = jnp.stack((keys, values)).reshape((2,) + tile_shape)
    sources = {0: own_pairs}
    for offset in offsets:
        fetched = shifted(jnp.stack((keys, values)), "ctx", offset)
        sources[offset] = fetched.reshape((2,) + tile_shape)
    empty_tile = jnp.zeros((2, BLOCK, heads_here, HD), jnp.bfloat16)
    gathered = []
    for source, key_index in routing:
        if source in sources:
            gathered.append(sources[source][:, key_index])
        else:
            gathered.append(empty_tile)
    pair_kv = jnp.stack(gathered, axis=1)
    key_tiles = pair_kv[0]
    value_tiles = pair_kv[1]
    key_stack = key_tiles.reshape((blocks, slot_count) + tile_shape[1:])
    value_stack = value_tiles.reshape((blocks, slot_count) + tile_shape[1:])
    own_rows = lax.dynamic_slice_in_dim(pattern, device_index * blocks, blocks, 0)
    positions = jnp.arange(BLOCK)
    causal = positions[None, :] <= positions[:, None]
    self_slot = jnp.arange(slot_count) == LEVELS
    tile_keep = (own_rows >= 0)[:, :, None, None] & (
        jnp.logical_not(self_slot)[None, :, None, None] | causal[None, None]
    )
    scores = (
        jnp.einsum("bqhd,bskhd->bhqsk", query_blocks, key_stack, preferred_element_type=jnp.float32)
        * score_scale
    )
    scores = jnp.where(jnp.transpose(tile_keep, (0, 2, 1, 3))[:, None], scores, NEG_BIG)
    highest = jnp.max(scores, axis=(3, 4))
    log_total = highest + jnp.log(jnp.sum(jnp.exp(scores - highest[..., None, None]), axis=(3, 4)))
    prob_stack = jnp.exp(scores - log_total[..., None, None]).astype(jnp.bfloat16)
    attention = jnp.einsum(
        "bhqsk,bskhd->bqhd", prob_stack, value_stack, preferred_element_type=jnp.float32
    ).astype(jnp.bfloat16)
    attn_wide = attention.reshape(tokens_here, heads_here * HD).astype(jnp.float32)
    square_sum = lax.psum(jnp.sum(attn_wide * attn_wide, axis=1), "head")
    inverse = lax.rsqrt(square_sum / WIDTH + EPSILON)
    normed = (attn_wide * inverse[:, None]).astype(jnp.bfloat16)
    upstream_wide = upstream.astype(jnp.float32)
    cross_term = lax.psum(jnp.sum(upstream_wide * attn_wide, axis=1), "head")
    grad_attn = (
        inverse[:, None] * upstream_wide - attn_wide * (inverse**3 * cross_term / WIDTH)[:, None]
    ).astype(jnp.bfloat16)
    row_delta = jnp.sum(
        (grad_attn.astype(jnp.float32) * attn_wide).reshape(tokens_here, heads_here, HD), axis=2
    )
    row_delta = jnp.transpose(row_delta.reshape(blocks, BLOCK, heads_here), (0, 2, 1))

    def spread(array):
        return jnp.broadcast_to(array[:, None], (blocks, slot_count) + array.shape[1:]).reshape(
            (pair_count,) + array.shape[1:]
        )

    grad_blocks = grad_attn.reshape(tile_shape)
    query_pairs = spread(query_blocks)
    grad_pairs = spread(grad_blocks)
    keep_pairs = tile_keep.reshape(pair_count, BLOCK, BLOCK)
    dscore, prob_pairs = pair_grads(
        query_pairs,
        grad_pairs,
        spread(log_total),
        spread(row_delta),
        key_tiles,
        value_tiles,
        keep_pairs,
        score_scale,
    )
    grad_query = jnp.einsum(
        "phqk,pkhd->pqhd", dscore, key_tiles, preferred_element_type=jnp.float32
    )
    grad_query = jnp.sum(grad_query.reshape((blocks, slot_count) + tile_shape[1:]), axis=1)
    grad_queries = grad_query.astype(jnp.bfloat16).reshape(tokens_here, heads_here * HD)
    local_rows = [row_index for row_index in range(pair_count) if routing[row_index][0] == 0]
    chosen = jnp.array(local_rows, jnp.int32)
    local_terms = key_grads(
        dscore[chosen], prob_pairs[chosen], query_pairs[chosen], grad_pairs[chosen]
    )
    key_sum = collect(local_terms, [routing[row_index][1] for row_index in local_rows], blocks)
    for offset in offsets:
        remote_rows = [
            row_index for row_index in range(pair_count) if routing[row_index][0] == offset
        ]
        chosen = jnp.array(remote_rows, jnp.int32)
        remote_terms = key_grads(
            dscore[chosen], prob_pairs[chosen], query_pairs[chosen], grad_pairs[chosen]
        )
        outgoing = collect(
            remote_terms, [routing[row_index][1] for row_index in remote_rows], blocks
        )
        key_sum = key_sum + shifted(for_sending(outgoing), "ctx", -offset).astype(outgoing.dtype)
    grad_keys = key_sum[0].astype(jnp.bfloat16).reshape(tokens_here, heads_here * HD)
    grad_values = key_sum[1].astype(jnp.bfloat16).reshape(tokens_here, heads_here * HD)
    return (normed, grad_queries, grad_keys, grad_values)


def solution(mesh):
    return jax.shard_map(
        shards,
        mesh=mesh,
        in_specs=(P("ctx", "head"), P("ctx", "head"), P("ctx", "head"), P(), P("ctx", "head")),
        out_specs=(P("ctx", "head"), P("ctx", "head"), P("ctx", "head"), P("ctx", "head")),
        check_vma=False,
    )
```

profile of v0, /device:TPU:64, one launch (start us, length us, event | category | flops | bytes accessed | tf_op | source)
XLA Modules:
  0.0 228.5 jit_solution(5779457081914570927)
XLA Ops:
  3.0 8.1 %collective-permute-start.5 = (bf16[2,128,1024]{1,2,0:T(8,128)(2,1)S(1)}, bf16[2,128,1024]{1,2,0:T(8,128)(2,1)}, u32[]{:S(2)}, u32[]{:S(2)}) collective-permute-start(bf16[2,128,1024]{1,2,0:T(8,128)(2,1)S(1)} %pad_maximum_fusion), channel_id=1, source_target_pairs={{0,128},{4,132},{8,136},{12,140},{16,144},{20,148},{24,152},{28,15... | collective-permute-start | bytes 1572872 | tf_op jit(solution)/shard_map/ppermute | solution.py:17
  11.1 1.9 collective-permute-start.4
  13.0 2.9 %collective-permute-start.3 = (bf16[2,128,1024]{1,2,0:T(8,128)(2,1)S(1)}, bf16[2,128,1024]{1,2,0:T(8,128)(2,1)S(1)}, u32[]{:S(2)}, u32[]{:S(2)}) collective-permute-start(bf16[2,128,1024]{1,2,0:T(8,128)(2,1)S(1)} %pad_maximum_fusion), channel_id=1, source_target_pairs={{0,32},{4,36},{8,40},{12,44},{16,48},{20,52},{24,56},{28,60},{32,6... | collective-permute-start | bytes 1572872 | tf_op jit(solution)/shard_map/ppermute | solution.py:17
  15.9 4.9 %collective-permute-start.2 = (bf16[2,128,1024]{1,2,0:T(8,128)(2,1)S(1)}, bf16[2,128,1024]{1,2,0:T(8,128)(2,1)S(1)}, u32[]{:S(2)}, u32[]{:S(2)}) collective-permute-start(bf16[2,128,1024]{1,2,0:T(8,128)(2,1)S(1)} %pad_maximum_fusion), channel_id=1, source_target_pairs={{0,16},{4,20},{8,24},{12,28},{16,32},{20,36},{24,40},{28,44},{32,4... | collective-permute-start | bytes 1572872 | tf_op jit(solution)/shard_map/ppermute | solution.py:17
  20.9 2.5 %collective-permute-start.1 = (bf16[2,128,1024]{1,2,0:T(8,128)(2,1)S(1)}, bf16[2,128,1024]{1,2,0:T(8,128)(2,1)S(1)}, u32[]{:S(2)}, u32[]{:S(2)}) collective-permute-start(bf16[2,128,1024]{1,2,0:T(8,128)(2,1)S(1)} %pad_maximum_fusion), channel_id=1, source_target_pairs={{0,8},{4,12},{8,16},{12,20},{16,24},{20,28},{24,32},{28,36},{32,40... | collective-permute-start | bytes 1572872 | tf_op jit(solution)/shard_map/ppermute | solution.py:17
  24.3 10.3 %collective-permute-done.5 = bf16[2,128,1024]{1,2,0:T(8,128)(2,1)} collective-permute-done((bf16[2,128,1024]{1,2,0:T(8,128)(2,1)S(1)}, bf16[2,128,1024]{1,2,0:T(8,128)(2,1)}, u32[]{:S(2)}, u32[]{:S(2)}) %collective-permute-start.5) | collective-permute-done | bytes 524320 | tf_op jit(solution)/shard_map/ppermute | solution.py:17
  34.7 1.9 collective-permute-start
  39.2 1.7 copy.199
  40.9 1.5 or_and_fusion
  43.1 1.3 copy.129
  44.5 11.9 %collective-permute-done.4 = bf16[2,128,1024]{1,2,0:T(8,128)(2,1)S(1)} collective-permute-done((bf16[2,128,1024]{1,2,0:T(8,128)(2,1)S(1)}, bf16[2,128,1024]{1,2,0:T(8,128)(2,1)S(1)}, u32[]{:S(2)}, u32[]{:S(2)}) %collective-permute-start.4) | collective-permute-done | bytes 524320 | tf_op jit(solution)/shard_map/ppermute | solution.py:17
  57.1 1.3 copy.128
  58.4 8.1 %collective-permute-done.3 = bf16[2,128,1024]{1,2,0:T(8,128)(2,1)S(1)} collective-permute-done((bf16[2,128,1024]{1,2,0:T(8,128)(2,1)S(1)}, bf16[2,128,1024]{1,2,0:T(8,128)(2,1)S(1)}, u32[]{:S(2)}, u32[]{:S(2)}) %collective-permute-start.3) | collective-permute-done | bytes 524320 | tf_op jit(solution)/shard_map/ppermute | solution.py:17
  68.7 2.5 %collective-permute-done.2 = bf16[2,128,1024]{1,2,0:T(8,128)(2,1)S(1)} collective-permute-done((bf16[2,128,1024]{1,2,0:T(8,128)(2,1)S(1)}, bf16[2,128,1024]{1,2,0:T(8,128)(2,1)S(1)}, u32[]{:S(2)}, u32[]{:S(2)}) %collective-permute-start.2) | collective-permute-done | bytes 524320 | tf_op jit(solution)/shard_map/ppermute | solution.py:17
  73.3 8.9 %collective-permute-done.1 = bf16[2,128,1024]{1,2,0:T(8,128)(2,1)S(1)} collective-permute-done((bf16[2,128,1024]{1,2,0:T(8,128)(2,1)S(1)}, bf16[2,128,1024]{1,2,0:T(8,128)(2,1)S(1)}, u32[]{:S(2)}, u32[]{:S(2)}) %collective-permute-start.1) | collective-permute-done | bytes 524320 | tf_op jit(solution)/shard_map/ppermute | solution.py:17
  84.3 3.5 %collective-permute-done = bf16[2,128,1024]{1,2,0:T(8,128)(2,1)} collective-permute-done((bf16[2,128,1024]{1,2,0:T(8,128)(2,1)S(1)}, bf16[2,128,1024]{1,2,0:T(8,128)(2,1)}, u32[]{:S(2)}, u32[]{:S(2)}) %collective-permute-start) | collective-permute-done | bytes 524320 | tf_op jit(solution)/shard_map/ppermute | solution.py:17
  87.9 1.3 copy.124
  90.3 2.0 slice_bitcast_fusion.1
  94.1 2.4 %multiply_reduce_fusion = (f32[128]{0:T(128)S(1)}, f32[8,128,128]{2,1,0:T(8,128)}) fusion(f32[8,8,128,128]{3,2,1,0:T(8,128)S(1)} %get-tuple-element.336, f32[8,128]{1,0:T(8,128)S(1)} %log_add_fusion, pred[128,8,128]{0,2,1:T(8,128)(4,1)S(1)} %and_bitcast_fusion, bf16[2,8,128,8,128]{4,2,1,3,0:T(8,128)(2,1)S(1)} %maximum_dynamic-update-slice_fusion), kind=kOutput, calls=%fused_computation.76 | convolution fusion | flops 273153920 | bytes 6951424 | tf_op jit(solution)/shard_map/bhqsk,bskhd->bqhd/dot_general | solution.py:123
  97.9 10.9 %all-reduce = (f32[128]{0:T(128)S(1)}, f32[128]{0:T(128)S(1)}) all-reduce(f32[128]{0:T(128)S(1)} %get-tuple-element.337, f32[128]{0:T(128)S(1)} %fusion.45), channel_id=1, replica_groups=mesh['ctx'=64,'head'=4] {'head'}, use_global_device_ids=true, to_apply=%region_3.4 | all-reduce | flops 256 | bytes 2048 | tf_op jit(solution)/shard_map/psum | solution.py:127
  110.2 3.3 %fusion.3 = (bf16[8,8,128,128]{3,2,1,0:T(8,128)(2,1)S(1)}, f32[8,8,128,128]{2,3,1,0:T(8,128)S(1)}) fusion(f32[8,128]{1,0:T(8,128)S(1)} %log_add_fusion, pred[8,128,128]{2,1,0:T(8,128)(4,1)S(1)} %copy-done.13, bf16[128,8,128]{2,0,1:T(8,128)(2,1)} %copy_bitcast_fusion.1, bf16[8,128,8,128]{3,1,0,2:T(8,128)(2,1)} %get-tuple-element.327), kind=kOutput, calls=%fused_computation.8 | convolution fusion | flops 272629760 | bytes 8785920 | tf_op jit(solution)/shard_map/pqhd,pkhd->phqk/dot_general | solution.py:42
  113.5 2.2 multiply_convert_fusion
  118.6 2.2 collective-permute-start.6
  121.6 1.9 collective-permute-start.7
  124.4 1.9 collective-permute-start.8
  127.1 1.9 collective-permute-start.9
  129.9 1.9 collective-permute-start.10
  138.7 11.2 %collective-permute-done.7 = bf16[2,1,128,8,128]{2,4,3,1,0:T(8,128)(2,1)S(1)} collective-permute-done((bf16[2,1,128,8,128]{2,4,3,1,0:T(8,128)(2,1)}, bf16[2,1,128,8,128]{2,4,3,1,0:T(8,128)(2,1)S(1)}, u32[]{:S(2)}, u32[]{:S(2)}) %collective-permute-start.7) | collective-permute-done | bytes 524320 | tf_op jit(solution)/shard_map/ppermute | solution.py:17
  149.9 11.2 %collective-permute-done.8 = bf16[2,1,128,8,128]{2,4,3,1,0:T(8,128)(2,1)S(1)} collective-permute-done((bf16[2,1,128,8,128]{2,4,3,1,0:T(8,128)(2,1)}, bf16[2,1,128,8,128]{2,4,3,1,0:T(8,128)(2,1)S(1)}, u32[]{:S(2)}, u32[]{:S(2)}) %collective-permute-start.8) | collective-permute-done | bytes 524320 | tf_op jit(solution)/shard_map/ppermute | solution.py:17
  161.1 23.4 %collective-permute-done.9 = bf16[2,1,128,8,128]{2,4,3,1,0:T(8,128)(2,1)S(1)} collective-permute-done((bf16[2,1,128,8,128]{2,4,3,1,0:T(8,128)(2,1)}, bf16[2,1,128,8,128]{2,4,3,1,0:T(8,128)(2,1)S(1)}, u32[]{:S(2)}, u32[]{:S(2)}) %collective-permute-start.9) | collective-permute-done | bytes 524320 | tf_op jit(solution)/shard_map/ppermute | solution.py:17
  184.6 40.6 %collective-permute-done.10 = bf16[2,1,128,8,128]{2,4,3,1,0:T(8,128)(2,1)S(1)} collective-permute-done((bf16[2,1,128,8,128]{2,4,3,1,0:T(8,128)(2,1)}, bf16[2,1,128,8,128]{2,4,3,1,0:T(8,128)(2,1)S(1)}, u32[]{:S(2)}, u32[]{:S(2)}) %collective-permute-start.10) | collective-permute-done | bytes 524320 | tf_op jit(solution)/shard_map/ppermute | solution.py:17
  225.1 1.6 fusion.40
  (93 shorter events, 34.0 us)
Async XLA Ops:
  0.6 41.8 %copy-start = (bf16[128,1024]{1,0:T(8,128)(2,1)S(1)}, bf16[128,1024]{1,0:T(8,128)(2,1)}, u32[]{:S(2)}) copy-start(bf16[128,1024]{1,0:T(8,128)(2,1)} %param.12) | copy-start | bytes 786436
  3.0 31.7 %collective-permute-start.5 = (bf16[2,128,1024]{1,2,0:T(8,128)(2,1)S(1)}, bf16[2,128,1024]{1,2,0:T(8,128)(2,1)}, u32[]{:S(2)}, u32[]{:S(2)}) collective-permute-start(bf16[2,128,1024]{1,2,0:T(8,128)(2,1)S(1)} %pad_maximum_fusion), channel_id=1, source_target_pairs={{0,128},{4,132},{8,136},{12,140},{16,144},{20,148},{24,152},{28,15... | collective-permute-start | bytes 1572872 | tf_op jit(solution)/shard_map/ppermute | solution.py:17
  11.1 45.2 %collective-permute-start.4 = (bf16[2,128,1024]{1,2,0:T(8,128)(2,1)S(1)}, bf16[2,128,1024]{1,2,0:T(8,128)(2,1)S(1)}, u32[]{:S(2)}, u32[]{:S(2)}) collective-permute-start(bf16[2,128,1024]{1,2,0:T(8,128)(2,1)S(1)} %pad_maximum_fusion), channel_id=1, source_target_pairs={{0,64},{4,68},{8,72},{12,76},{16,80},{20,84},{24,88},{28,92},{32,9... | collective-permute-start | bytes 1572872 | tf_op jit(solution)/shard_map/ppermute | solution.py:17
  13.0 53.6 %collective-permute-start.3 = (bf16[2,128,1024]{1,2,0:T(8,128)(2,1)S(1)}, bf16[2,128,1024]{1,2,0:T(8,128)(2,1)S(1)}, u32[]{:S(2)}, u32[]{:S(2)}) collective-permute-start(bf16[2,128,1024]{1,2,0:T(8,128)(2,1)S(1)} %pad_maximum_fusion), channel_id=1, source_target_pairs={{0,32},{4,36},{8,40},{12,44},{16,48},{20,52},{24,56},{28,60},{32,6... | collective-permute-start | bytes 1572872 | tf_op jit(solution)/shard_map/ppermute | solution.py:17
  15.9 55.2 %collective-permute-start.2 = (bf16[2,128,1024]{1,2,0:T(8,128)(2,1)S(1)}, bf16[2,128,1024]{1,2,0:T(8,128)(2,1)S(1)}, u32[]{:S(2)}, u32[]{:S(2)}) collective-permute-start(bf16[2,128,1024]{1,2,0:T(8,128)(2,1)S(1)} %pad_maximum_fusion), channel_id=1, source_target_pairs={{0,16},{4,20},{8,24},{12,28},{16,32},{20,36},{24,40},{28,44},{32,4... | collective-permute-start | bytes 1572872 | tf_op jit(solution)/shard_map/ppermute | solution.py:17
  20.9 61.3 %collective-permute-start.1 = (bf16[2,128,1024]{1,2,0:T(8,128)(2,1)S(1)}, bf16[2,128,1024]{1,2,0:T(8,128)(2,1)S(1)}, u32[]{:S(2)}, u32[]{:S(2)}) collective-permute-start(bf16[2,128,1024]{1,2,0:T(8,128)(2,1)S(1)} %pad_maximum_fusion), channel_id=1, source_target_pairs={{0,8},{4,12},{8,16},{12,20},{16,24},{20,28},{24,32},{28,36},{32,40... | collective-permute-start | bytes 1572872 | tf_op jit(solution)/shard_map/ppermute | solution.py:17
  24.3 12.3 %copy-start.14 = (pred[8]{0:T(512)(128)(4,1)}, pred[8]{0:T(512)(128)(4,1)S(1)}, u32[]{:S(2)}) copy-start(pred[8]{0:T(512)(128)(4,1)S(1)} %fusion.48) | copy-start | bytes 28
  24.3 12.3 %copy-start.15 = (pred[8]{0:T(512)(128)(4,1)}, pred[8]{0:T(512)(128)(4,1)S(1)}, u32[]{:S(2)}) copy-start(pred[8]{0:T(512)(128)(4,1)S(1)} %compare_not_fusion) | copy-start | bytes 28
  34.7 53.2 %collective-permute-start = (bf16[2,128,1024]{1,2,0:T(8,128)(2,1)S(1)}, bf16[2,128,1024]{1,2,0:T(8,128)(2,1)}, u32[]{:S(2)}, u32[]{:S(2)}) collective-permute-start(bf16[2,128,1024]{1,2,0:T(8,128)(2,1)S(1)} %pad_maximum_fusion), channel_id=1, source_target_pairs={{0,4},{4,8},{8,12},{12,16},{16,20},{20,24},{24,28},{28,32},{32,36}... | collective-permute-start | bytes 1572872 | tf_op jit(solution)/shard_map/ppermute | solution.py:17
  56.3 0.8 copy-start.11
  66.6 0.8 copy-start.10
  71.2 0.8 copy-start.9
  82.2 0.8 copy-start.8
  89.2 1.0 copy-start.6
  89.2 1.0 copy-start.7
  90.3 3.8 %copy-start.1 = (bf16[2,8,128,8,128]{4,2,1,3,0:T(8,128)(2,1)}, bf16[2,8,128,8,128]{4,2,1,3,0:T(8,128)(2,1)S(1)}, u32[]{:S(2)}) copy-start(bf16[2,8,128,8,128]{4,2,1,3,0:T(8,128)(2,1)S(1)} %maximum_dynamic-update-slice_fusion) | copy-start | bytes 12582916
  90.3 2.0 copy-start.12
  94.1 3.7 %copy-start.5 = (bf16[128,1024]{1,0:T(8,128)(2,1)S(1)}, bf16[128,1024]{1,0:T(8,128)(2,1)}, u32[]{:S(2)}) copy-start(bf16[128,1024]{1,0:T(8,128)(2,1)} %param.16) | copy-start | bytes 786436
  96.4 13.7 %copy-start.13 = (pred[8,128,128]{2,1,0:T(8,128)(4,1)S(1)}, pred[8,128,128]{2,1,0:T(8,128)(4,1)}, u32[]{:S(2)}) copy-start(pred[8,128,128]{2,1,0:T(8,128)(4,1)} %or_and_fusion) | copy-start | bytes 393220
  113.4 18.7 %copy-start.3 = (bf16[8,8,128,128]{3,2,1,0:T(8,128)(2,1)}, bf16[8,8,128,128]{3,2,1,0:T(8,128)(2,1)S(1)}, u32[]{:S(2)}) copy-start(bf16[8,8,128,128]{3,2,1,0:T(8,128)(2,1)S(1)} %get-tuple-element.339) | copy-start | bytes 6291460
  115.6 18.9 %copy-start.4 = (bf16[8,8,128,128]{3,2,1,0:T(8,128)(2,1)}, bf16[8,8,128,128]{3,2,1,0:T(8,128)(2,1)S(1)}, u32[]{:S(2)}) copy-start(bf16[8,8,128,128]{3,2,1,0:T(8,128)(2,1)S(1)} %multiply_convert_fusion) | copy-start | bytes 6291460
  118.2 16.4 %copy-start.2 = (bf16[2,8,128,8,128]{4,2,1,3,0:T(8,128)(2,1)S(1)}, bf16[2,8,128,8,128]{4,2,1,3,0:T(8,128)(2,1)}, u32[]{:S(2)}) copy-start(bf16[2,8,128,8,128]{4,2,1,3,0:T(8,128)(2,1)} %copy-done.1) | copy-start | bytes 12582916
  118.6 14.7 %collective-permute-start.6 = (bf16[2,1,128,8,128]{2,4,3,1,0:T(8,128)(2,1)S(1)}, bf16[2,1,128,8,128]{2,4,3,1,0:T(8,128)(2,1)S(1)}, u32[]{:S(2)}, u32[]{:S(2)}) collective-permute-start(bf16[2,1,128,8,128]{2,4,3,1,0:T(8,128)(2,1)S(1)} %pad_maximum_fusion.1), channel_id=1, source_target_pairs={{4,0},{8,4},{12,8},{16,12},{20,16},{24,20},{28,24},{32,28},{36,32}... | collective-permute-start | bytes 1572872 | tf_op jit(solution)/shard_map/ppermute | solution.py:17
  121.6 28.3 %collective-permute-start.7 = (bf16[2,1,128,8,128]{2,4,3,1,0:T(8,128)(2,1)}, bf16[2,1,128,8,128]{2,4,3,1,0:T(8,128)(2,1)S(1)}, u32[]{:S(2)}, u32[]{:S(2)}) collective-permute-start(bf16[2,1,128,8,128]{2,4,3,1,0:T(8,128)(2,1)} %pad_maximum_fusion.2), channel_id=1, source_target_pairs={{8,0},{12,4},{16,8},{20,12},{24,16},{28,20},{32,24},{36,28},{40,32... | collective-permute-start | bytes 1572872 | tf_op jit(solution)/shard_map/ppermute | solution.py:17
  124.4 36.8 %collective-permute-start.8 = (bf16[2,1,128,8,128]{2,4,3,1,0:T(8,128)(2,1)}, bf16[2,1,128,8,128]{2,4,3,1,0:T(8,128)(2,1)S(1)}, u32[]{:S(2)}, u32[]{:S(2)}) collective-permute-start(bf16[2,1,128,8,128]{2,4,3,1,0:T(8,128)(2,1)} %pad_maximum_fusion.3), channel_id=1, source_target_pairs={{16,0},{20,4},{24,8},{28,12},{32,16},{36,20},{40,24},{44,28},{48,3... | collective-permute-start | bytes 1572872 | tf_op jit(solution)/shard_map/ppermute | solution.py:17
  127.1 57.4 %collective-permute-start.9 = (bf16[2,1,128,8,128]{2,4,3,1,0:T(8,128)(2,1)}, bf16[2,1,128,8,128]{2,4,3,1,0:T(8,128)(2,1)S(1)}, u32[]{:S(2)}, u32[]{:S(2)}) collective-permute-start(bf16[2,1,128,8,128]{2,4,3,1,0:T(8,128)(2,1)} %pad_maximum_fusion.4), channel_id=1, source_target_pairs={{32,0},{36,4},{40,8},{44,12},{48,16},{52,20},{56,24},{60,28},{64,3... | collective-permute-start | bytes 1572872 | tf_op jit(solution)/shard_map/ppermute | solution.py:17
  129.9 95.2 %collective-permute-start.10 = (bf16[2,1,128,8,128]{2,4,3,1,0:T(8,128)(2,1)}, bf16[2,1,128,8,128]{2,4,3,1,0:T(8,128)(2,1)S(1)}, u32[]{:S(2)}, u32[]{:S(2)}) collective-permute-start(bf16[2,1,128,8,128]{2,4,3,1,0:T(8,128)(2,1)} %pad_maximum_fusion.5), channel_id=1, source_target_pairs={{64,0},{68,4},{72,8},{76,12},{80,16},{84,20},{88,24},{92,28},{96,3... | collective-permute-start | bytes 1572872 | tf_op jit(solution)/shard_map/ppermute | solution.py:17
  133.3 91.8 %collective-permute-start.11 = (bf16[2,1,128,8,128]{2,4,3,1,0:T(8,128)(2,1)}, bf16[2,1,128,8,128]{2,4,3,1,0:T(8,128)(2,1)}, u32[]{:S(2)}, u32[]{:S(2)}) collective-permute-start(bf16[2,1,128,8,128]{2,4,3,1,0:T(8,128)(2,1)} %pad_maximum_fusion.6), channel_id=1, source_target_pairs={{128,0},{132,4},{136,8},{140,12},{144,16},{148,20},{152,24},{156,2... | collective-permute-start | bytes 1572872 | tf_op jit(solution)/shard_map/ppermute | solution.py:17
where the time goes:
time: 230 us; the launch traced here: 228 us
  waiting for transfers between devices  132 us (57%)
  starting transfers between devices  33.4 us (15%)
  local copies, waits for them, and re-layouts  25.3 us (11%)
  matrix products  15.2 us (7%)
  blocking collectives  10.9 us (5%)
  other arithmetic  10.8 us (5%)
    ppermute x12, waiting for transfers between devices, shifted(): return lax.ppermute(block, axis, route)  132 us
    ppermute x12, starting transfers between devices, shifted(): return lax.ppermute(block, axis, route)  33.4 us
    psum x1, blocking collectives, shards(): square_sum = lax.psum(jnp.sum(attn_wide * attn_wide, axis=1), 'head')  10.9 us
    unnamed x46, local copies, waits for them, and re-layouts  10.8 us
    another operation x6, local copies, waits for them, and re-layouts, shards(): pair_kv = jnp.stack(gathered, axis=1)  7.87 us
  transfers between devices with their start and end apart: 12, of which 10 were waited for; matrix products, arithmetic and copies ran while one was open for 10% of the time, Pallas kernels for 0%

commit v1 on v0

--- a/solution.py
+++ b/solution.py
@@ -1,3 +1,4 @@
+import functools
 import jax
 import jax.numpy as jnp
 from jax import lax
@@ -9,6 +10,14 @@
 WIDTH = 4096
 NEG_BIG = -1e30
 EPSILON = 1e-06
+
+
+def supply_marks(obj, lane_axis):
+    z2 = lax.all_gather(obj, axis_name=lane_axis).sum(axis=0)
+    return z2
+
+
+things_attach = functools.partial(supply_marks, lane_axis="head")
 
 
 def shifted(block, axis, distance):
@@ -124,7 +133,7 @@
         "bhqsk,bskhd->bqhd", prob_stack, value_stack, preferred_element_type=jnp.float32
     ).astype(jnp.bfloat16)
     attn_wide = attention.reshape(tokens_here, heads_here * HD).astype(jnp.float32)
-    square_sum = lax.psum(jnp.sum(attn_wide * attn_wide, axis=1), "head")
+    square_sum = things_attach(jnp.sum(attn_wide * attn_wide, axis=1))
     inverse = lax.rsqrt(square_sum / WIDTH + EPSILON)
     normed = (attn_wide * inverse[:, None]).astype(jnp.bfloat16)
     upstream_wide = upstream.astype(jnp.float32)

time: 230 us -> 237 us (1.030)
  blocking collectives: 10.9 us -> 17.8 us
    all_gather x0 -> x1, blocking collectives: none -> 7.09 us  [supply_marks(): z2 = lax.all_gather(obj, axis_name=lane_axis).sum(axis=0)]
where the time goes in v1:
time: 237 us; the launch traced here: 235 us
  waiting for transfers between devices  132 us (56%)
  starting transfers between devices  33.4 us (14%)
  local copies, waits for them, and re-layouts  25.2 us (11%)
  blocking collectives  17.8 us (8%)
  matrix products  15.3 us (6%)
  other arithmetic  10.8 us (5%)
    ppermute x12, waiting for transfers between devices, shifted(): return lax.ppermute(block, axis, route)  132 us
    ppermute x12, starting transfers between devices, shifted(): return lax.ppermute(block, axis, route)  33.4 us
    unnamed x46, local copies, waits for them, and re-layouts  10.8 us
    psum x1, blocking collectives, shards(): cross_term = lax.psum(jnp.sum(upstream_wide * attn_wide, axis=1), 'head')  10.7 us
    another operation x6, local copies, waits for them, and re-layouts, shards(): pair_kv = jnp.stack(gathered, axis=1)  7.87 us
    all_gather x1, blocking collectives, supply_marks(): z2 = lax.all_gather(obj, axis_name=lane_axis).sum(axis=0)  7.09 us
  transfers between devices with their start and end apart: 12, of which 10 were waited for; matrix products, arithmetic and copies ran while one was open for 10% of the time, Pallas kernels for 0%

profile of v1, /device:TPU:64, one launch (start us, length us, event | category | flops | bytes accessed | tf_op | source)
XLA Modules:
  0.0 235.4 jit_solution(16415817316279422817)
XLA Ops:
  3.0 8.1 %collective-permute-start.5 = (bf16[2,128,1024]{1,2,0:T(8,128)(2,1)S(1)}, bf16[2,128,1024]{1,2,0:T(8,128)(2,1)}, u32[]{:S(2)}, u32[]{:S(2)}) collective-permute-start(bf16[2,128,1024]{1,2,0:T(8,128)(2,1)S(1)} %pad_maximum_fusion), channel_id=1, source_target_pairs={{0,128},{4,132},{8,136},{12,140},{16,144},{20,148},{24,152},{28,15... | collective-permute-start | bytes 1572872 | tf_op jit(solution)/shard_map/ppermute | solution.py:26
  11.1 1.9 collective-permute-start.4
  13.0 2.9 %collective-permute-start.3 = (bf16[2,128,1024]{1,2,0:T(8,128)(2,1)S(1)}, bf16[2,128,1024]{1,2,0:T(8,128)(2,1)S(1)}, u32[]{:S(2)}, u32[]{:S(2)}) collective-permute-start(bf16[2,128,1024]{1,2,0:T(8,128)(2,1)S(1)} %pad_maximum_fusion), channel_id=1, source_target_pairs={{0,32},{4,36},{8,40},{12,44},{16,48},{20,52},{24,56},{28,60},{32,6... | collective-permute-start | bytes 1572872 | tf_op jit(solution)/shard_map/ppermute | solution.py:26
  15.9 4.9 %collective-permute-start.2 = (bf16[2,128,1024]{1,2,0:T(8,128)(2,1)S(1)}, bf16[2,128,1024]{1,2,0:T(8,128)(2,1)S(1)}, u32[]{:S(2)}, u32[]{:S(2)}) collective-permute-start(bf16[2,128,1024]{1,2,0:T(8,128)(2,1)S(1)} %pad_maximum_fusion), channel_id=1, source_target_pairs={{0,16},{4,20},{8,24},{12,28},{16,32},{20,36},{24,40},{28,44},{32,4... | collective-permute-start | bytes 1572872 | tf_op jit(solution)/shard_map/ppermute | solution.py:26
  20.9 2.5 %collective-permute-start.1 = (bf16[2,128,1024]{1,2,0:T(8,128)(2,1)S(1)}, bf16[2,128,1024]{1,2,0:T(8,128)(2,1)S(1)}, u32[]{:S(2)}, u32[]{:S(2)}) collective-permute-start(bf16[2,128,1024]{1,2,0:T(8,128)(2,1)S(1)} %pad_maximum_fusion), channel_id=1, source_target_pairs={{0,8},{4,12},{8,16},{12,20},{16,24},{20,28},{24,32},{28,36},{32,40... | collective-permute-start | bytes 1572872 | tf_op jit(solution)/shard_map/ppermute | solution.py:26
  24.3 10.3 %collective-permute-done.5 = bf16[2,128,1024]{1,2,0:T(8,128)(2,1)} collective-permute-done((bf16[2,128,1024]{1,2,0:T(8,128)(2,1)S(1)}, bf16[2,128,1024]{1,2,0:T(8,128)(2,1)}, u32[]{:S(2)}, u32[]{:S(2)}) %collective-permute-start.5) | collective-permute-done | bytes 524320 | tf_op jit(solution)/shard_map/ppermute | solution.py:26
  34.7 1.9 collective-permute-start
  39.2 1.7 copy.199
  40.9 1.5 or_and_fusion
  43.1 1.3 copy.129
  44.5 11.9 %collective-permute-done.4 = bf16[2,128,1024]{1,2,0:T(8,128)(2,1)S(1)} collective-permute-done((bf16[2,128,1024]{1,2,0:T(8,128)(2,1)S(1)}, bf16[2,128,1024]{1,2,0:T(8,128)(2,1)S(1)}, u32[]{:S(2)}, u32[]{:S(2)}) %collective-permute-start.4) | collective-permute-done | bytes 524320 | tf_op jit(solution)/shard_map/ppermute | solution.py:26
  58.4 8.1 %collective-permute-done.3 = bf16[2,128,1024]{1,2,0:T(8,128)(2,1)S(1)} collective-permute-done((bf16[2,128,1024]{1,2,0:T(8,128)(2,1)S(1)}, bf16[2,128,1024]{1,2,0:T(8,128)(2,1)S(1)}, u32[]{:S(2)}, u32[]{:S(2)}) %collective-permute-start.3) | collective-permute-done | bytes 524320 | tf_op jit(solution)/shard_map/ppermute | solution.py:26
  68.7 2.5 %collective-permute-done.2 = bf16[2,128,1024]{1,2,0:T(8,128)(2,1)S(1)} collective-permute-done((bf16[2,128,1024]{1,2,0:T(8,128)(2,1)S(1)}, bf16[2,128,1024]{1,2,0:T(8,128)(2,1)S(1)}, u32[]{:S(2)}, u32[]{:S(2)}) %collective-permute-start.2) | collective-permute-done | bytes 524320 | tf_op jit(solution)/shard_map/ppermute | solution.py:26
  73.3 9.0 %collective-permute-done.1 = bf16[2,128,1024]{1,2,0:T(8,128)(2,1)S(1)} collective-permute-done((bf16[2,128,1024]{1,2,0:T(8,128)(2,1)S(1)}, bf16[2,128,1024]{1,2,0:T(8,128)(2,1)S(1)}, u32[]{:S(2)}, u32[]{:S(2)}) %collective-permute-start.1) | collective-permute-done | bytes 524320 | tf_op jit(solution)/shard_map/ppermute | solution.py:26
  84.3 3.5 %collective-permute-done = bf16[2,128,1024]{1,2,0:T(8,128)(2,1)} collective-permute-done((bf16[2,128,1024]{1,2,0:T(8,128)(2,1)S(1)}, bf16[2,128,1024]{1,2,0:T(8,128)(2,1)}, u32[]{:S(2)}, u32[]{:S(2)}) %collective-permute-start) | collective-permute-done | bytes 524320 | tf_op jit(solution)/shard_map/ppermute | solution.py:26
  87.9 1.3 copy.124
  90.3 2.0 slice_bitcast_fusion.1
  94.1 2.4 %multiply_reduce_fusion = (f32[128]{0:T(128)S(1)}, f32[8,128,128]{2,1,0:T(8,128)}) fusion(f32[8,8,128,128]{3,2,1,0:T(8,128)S(1)} %get-tuple-element.334, f32[8,128]{1,0:T(8,128)S(1)} %log_add_fusion, pred[128,8,128]{0,2,1:T(8,128)(4,1)S(1)} %and_bitcast_fusion, bf16[2,8,128,8,128]{4,2,1,3,0:T(8,128)(2,1)S(1)} %maximum_dynamic-update-slice_fusion), kind=kOutput, calls=%fused_computation.76 | convolution fusion | flops 273153920 | bytes 6951424 | tf_op jit(solution)/shard_map/bhqsk,bskhd->bqhd/dot_general | solution.py:132
  97.9 10.7 %psum.7 = f32[128]{0:T(128)S(1)} all-reduce(f32[128]{0:T(128)S(1)} %fusion.45), channel_id=1, replica_groups=mesh['ctx'=64,'head'=4] {'head'}, use_global_device_ids=true, to_apply=%region_5.6 | all-reduce | flops 128 | bytes 1024 | tf_op jit(solution)/shard_map/psum | solution.py:140
  108.6 7.1 %all-gather.1 = f32[4,1,128]{2,1,0:T(1,128)S(1)} all-gather(f32[1,1,128]{2,1,0:T(1,128)S(1)} %bitcast.289), channel_id=2, replica_groups=mesh['ctx'=64,'head'=4] {'head'}, dimensions={0}, use_global_device_ids=true | all-gather | bytes 2560 | tf_op jit(solution)/shard_map/all_gather | solution.py:16
  117.1 3.3 %fusion.3 = (bf16[8,8,128,128]{3,2,1,0:T(8,128)(2,1)S(1)}, f32[8,8,128,128]{2,3,1,0:T(8,128)S(1)}) fusion(f32[8,128]{1,0:T(8,128)S(1)} %log_add_fusion, pred[8,128,128]{2,1,0:T(8,128)(4,1)S(1)} %copy-done.13, bf16[128,8,128]{2,0,1:T(8,128)(2,1)} %copy_bitcast_fusion.1, bf16[8,128,8,128]{3,1,0,2:T(8,128)(2,1)} %get-tuple-element.325), kind=kOutput, calls=%fused_computation.8 | convolution fusion | flops 272629760 | bytes 8785920 | tf_op jit(solution)/shard_map/pqhd,pkhd->phqk/dot_general | solution.py:51
  120.4 2.2 multiply_convert_fusion
  125.5 2.2 collective-permute-start.6
  128.5 1.9 collective-permute-start.7
  131.3 1.9 collective-permute-start.8
  134.0 1.9 collective-permute-start.9
  136.8 1.9 collective-permute-start.10
  145.6 11.2 %collective-permute-done.7 = bf16[2,1,128,8,128]{2,4,3,1,0:T(8,128)(2,1)S(1)} collective-permute-done((bf16[2,1,128,8,128]{2,4,3,1,0:T(8,128)(2,1)}, bf16[2,1,128,8,128]{2,4,3,1,0:T(8,128)(2,1)S(1)}, u32[]{:S(2)}, u32[]{:S(2)}) %collective-permute-start.7) | collective-permute-done | bytes 524320 | tf_op jit(solution)/shard_map/ppermute | solution.py:26
  156.8 11.2 %collective-permute-done.8 = bf16[2,1,128,8,128]{2,4,3,1,0:T(8,128)(2,1)S(1)} collective-permute-done((bf16[2,1,128,8,128]{2,4,3,1,0:T(8,128)(2,1)}, bf16[2,1,128,8,128]{2,4,3,1,0:T(8,128)(2,1)S(1)}, u32[]{:S(2)}, u32[]{:S(2)}) %collective-permute-start.8) | collective-permute-done | bytes 524320 | tf_op jit(solution)/shard_map/ppermute | solution.py:26
  168.1 23.4 %collective-permute-done.9 = bf16[2,1,128,8,128]{2,4,3,1,0:T(8,128)(2,1)S(1)} collective-permute-done((bf16[2,1,128,8,128]{2,4,3,1,0:T(8,128)(2,1)}, bf16[2,1,128,8,128]{2,4,3,1,0:T(8,128)(2,1)S(1)}, u32[]{:S(2)}, u32[]{:S(2)}) %collective-permute-start.9) | collective-permute-done | bytes 524320 | tf_op jit(solution)/shard_map/ppermute | solution.py:26
  191.5 40.6 %collective-permute-done.10 = bf16[2,1,128,8,128]{2,4,3,1,0:T(8,128)(2,1)S(1)} collective-permute-done((bf16[2,1,128,8,128]{2,4,3,1,0:T(8,128)(2,1)}, bf16[2,1,128,8,128]{2,4,3,1,0:T(8,128)(2,1)S(1)}, u32[]{:S(2)}, u32[]{:S(2)}) %collective-permute-start.10) | collective-permute-done | bytes 524320 | tf_op jit(solution)/shard_map/ppermute | solution.py:26
  232.1 1.6 fusion.40
  (95 shorter events, 35.2 us)
Async XLA Ops:
  0.6 41.8 %copy-start = (bf16[128,1024]{1,0:T(8,128)(2,1)S(1)}, bf16[128,1024]{1,0:T(8,128)(2,1)}, u32[]{:S(2)}) copy-start(bf16[128,1024]{1,0:T(8,128)(2,1)} %param.12) | copy-start | bytes 786436
  3.0 31.7 %collective-permute-start.5 = (bf16[2,128,1024]{1,2,0:T(8,128)(2,1)S(1)}, bf16[2,128,1024]{1,2,0:T(8,128)(2,1)}, u32[]{:S(2)}, u32[]{:S(2)}) collective-permute-start(bf16[2,128,1024]{1,2,0:T(8,128)(2,1)S(1)} %pad_maximum_fusion), channel_id=1, source_target_pairs={{0,128},{4,132},{8,136},{12,140},{16,144},{20,148},{24,152},{28,15... | collective-permute-start | bytes 1572872 | tf_op jit(solution)/shard_map/ppermute | solution.py:26
  11.1 45.3 %collective-permute-start.4 = (bf16[2,128,1024]{1,2,0:T(8,128)(2,1)S(1)}, bf16[2,128,1024]{1,2,0:T(8,128)(2,1)S(1)}, u32[]{:S(2)}, u32[]{:S(2)}) collective-permute-start(bf16[2,128,1024]{1,2,0:T(8,128)(2,1)S(1)} %pad_maximum_fusion), channel_id=1, source_target_pairs={{0,64},{4,68},{8,72},{12,76},{16,80},{20,84},{24,88},{28,92},{32,9... | collective-permute-start | bytes 1572872 | tf_op jit(solution)/shard_map/ppermute | solution.py:26
  13.0 53.6 %collective-permute-start.3 = (bf16[2,128,1024]{1,2,0:T(8,128)(2,1)S(1)}, bf16[2,128,1024]{1,2,0:T(8,128)(2,1)S(1)}, u32[]{:S(2)}, u32[]{:S(2)}) collective-permute-start(bf16[2,128,1024]{1,2,0:T(8,128)(2,1)S(1)} %pad_maximum_fusion), channel_id=1, source_target_pairs={{0,32},{4,36},{8,40},{12,44},{16,48},{20,52},{24,56},{28,60},{32,6... | collective-permute-start | bytes 1572872 | tf_op jit(solution)/shard_map/ppermute | solution.py:26
  15.9 55.2 %collective-permute-start.2 = (bf16[2,128,1024]{1,2,0:T(8,128)(2,1)S(1)}, bf16[2,128,1024]{1,2,0:T(8,128)(2,1)S(1)}, u32[]{:S(2)}, u32[]{:S(2)}) collective-permute-start(bf16[2,128,1024]{1,2,0:T(8,128)(2,1)S(1)} %pad_maximum_fusion), channel_id=1, source_target_pairs={{0,16},{4,20},{8,24},{12,28},{16,32},{20,36},{24,40},{28,44},{32,4... | collective-permute-start | bytes 1572872 | tf_op jit(solution)/shard_map/ppermute | solution.py:26
  20.9 61.4 %collective-permute-start.1 = (bf16[2,128,1024]{1,2,0:T(8,128)(2,1)S(1)}, bf16[2,128,1024]{1,2,0:T(8,128)(2,1)S(1)}, u32[]{:S(2)}, u32[]{:S(2)}) collective-permute-start(bf16[2,128,1024]{1,2,0:T(8,128)(2,1)S(1)} %pad_maximum_fusion), channel_id=1, source_target_pairs={{0,8},{4,12},{8,16},{12,20},{16,24},{20,28},{24,32},{28,36},{32,40... | collective-permute-start | bytes 1572872 | tf_op jit(solution)/shard_map/ppermute | solution.py:26
  24.3 12.3 %copy-start.14 = (pred[8]{0:T(512)(128)(4,1)}, pred[8]{0:T(512)(128)(4,1)S(1)}, u32[]{:S(2)}) copy-start(pred[8]{0:T(512)(128)(4,1)S(1)} %fusion.48) | copy-start | bytes 28
  24.3 12.3 %copy-start.15 = (pred[8]{0:T(512)(128)(4,1)}, pred[8]{0:T(512)(128)(4,1)S(1)}, u32[]{:S(2)}) copy-start(pred[8]{0:T(512)(128)(4,1)S(1)} %compare_not_fusion) | copy-start | bytes 28
  34.7 53.2 %collective-permute-start = (bf16[2,128,1024]{1,2,0:T(8,128)(2,1)S(1)}, bf16[2,128,1024]{1,2,0:T(8,128)(2,1)}, u32[]{:S(2)}, u32[]{:S(2)}) collective-permute-start(bf16[2,128,1024]{1,2,0:T(8,128)(2,1)S(1)} %pad_maximum_fusion), channel_id=1, source_target_pairs={{0,4},{4,8},{8,12},{12,16},{16,20},{20,24},{24,28},{28,32},{32,36}... | collective-permute-start | bytes 1572872 | tf_op jit(solution)/shard_map/ppermute | solution.py:26
  56.3 0.8 copy-start.11
  66.6 0.8 copy-start.10
  71.2 0.8 copy-start.9
  82.2 0.8 copy-start.8
  89.2 1.0 copy-start.6
  89.2 1.0 copy-start.7
  90.3 3.7 %copy-start.1 = (bf16[2,8,128,8,128]{4,2,1,3,0:T(8,128)(2,1)}, bf16[2,8,128,8,128]{4,2,1,3,0:T(8,128)(2,1)S(1)}, u32[]{:S(2)}) copy-start(bf16[2,8,128,8,128]{4,2,1,3,0:T(8,128)(2,1)S(1)} %maximum_dynamic-update-slice_fusion) | copy-start | bytes 12582916
  90.3 2.0 copy-start.12
  94.0 3.7 %copy-start.5 = (bf16[128,1024]{1,0:T(8,128)(2,1)S(1)}, bf16[128,1024]{1,0:T(8,128)(2,1)}, u32[]{:S(2)}) copy-start(bf16[128,1024]{1,0:T(8,128)(2,1)} %param.16) | copy-start | bytes 786436
  96.4 20.6 %copy-start.13 = (pred[8,128,128]{2,1,0:T(8,128)(4,1)S(1)}, pred[8,128,128]{2,1,0:T(8,128)(4,1)}, u32[]{:S(2)}) copy-start(pred[8,128,128]{2,1,0:T(8,128)(4,1)} %or_and_fusion) | copy-start | bytes 393220
  120.4 18.6 %copy-start.3 = (bf16[8,8,128,128]{3,2,1,0:T(8,128)(2,1)}, bf16[8,8,128,128]{3,2,1,0:T(8,128)(2,1)S(1)}, u32[]{:S(2)}) copy-start(bf16[8,8,128,128]{3,2,1,0:T(8,128)(2,1)S(1)} %get-tuple-element.337) | copy-start | bytes 6291460
  122.6 18.9 %copy-start.4 = (bf16[8,8,128,128]{3,2,1,0:T(8,128)(2,1)}, bf16[8,8,128,128]{3,2,1,0:T(8,128)(2,1)S(1)}, u32[]{:S(2)}) copy-start(bf16[8,8,128,128]{3,2,1,0:T(8,128)(2,1)S(1)} %multiply_convert_fusion) | copy-start | bytes 6291460
  125.1 16.3 %copy-start.2 = (bf16[2,8,128,8,128]{4,2,1,3,0:T(8,128)(2,1)S(1)}, bf16[2,8,128,8,128]{4,2,1,3,0:T(8,128)(2,1)}, u32[]{:S(2)}) copy-start(bf16[2,8,128,8,128]{4,2,1,3,0:T(8,128)(2,1)} %copy-done.1) | copy-start | bytes 12582916
  125.5 14.7 %collective-permute-start.6 = (bf16[2,1,128,8,128]{2,4,3,1,0:T(8,128)(2,1)S(1)}, bf16[2,1,128,8,128]{2,4,3,1,0:T(8,128)(2,1)S(1)}, u32[]{:S(2)}, u32[]{:S(2)}) collective-permute-start(bf16[2,1,128,8,128]{2,4,3,1,0:T(8,128)(2,1)S(1)} %pad_maximum_fusion.1), channel_id=1, source_target_pairs={{4,0},{8,4},{12,8},{16,12},{20,16},{24,20},{28,24},{32,28},{36,32}... | collective-permute-start | bytes 1572872 | tf_op jit(solution)/shard_map/ppermute | solution.py:26
  128.5 28.3 %collective-permute-start.7 = (bf16[2,1,128,8,128]{2,4,3,1,0:T(8,128)(2,1)}, bf16[2,1,128,8,128]{2,4,3,1,0:T(8,128)(2,1)S(1)}, u32[]{:S(2)}, u32[]{:S(2)}) collective-permute-start(bf16[2,1,128,8,128]{2,4,3,1,0:T(8,128)(2,1)} %pad_maximum_fusion.2), channel_id=1, source_target_pairs={{8,0},{12,4},{16,8},{20,12},{24,16},{28,20},{32,24},{36,28},{40,32... | collective-permute-start | bytes 1572872 | tf_op jit(solution)/shard_map/ppermute | solution.py:26
  131.3 36.8 %collective-permute-start.8 = (bf16[2,1,128,8,128]{2,4,3,1,0:T(8,128)(2,1)}, bf16[2,1,128,8,128]{2,4,3,1,0:T(8,128)(2,1)S(1)}, u32[]{:S(2)}, u32[]{:S(2)}) collective-permute-start(bf16[2,1,128,8,128]{2,4,3,1,0:T(8,128)(2,1)} %pad_maximum_fusion.3), channel_id=1, source_target_pairs={{16,0},{20,4},{24,8},{28,12},{32,16},{36,20},{40,24},{44,28},{48,3... | collective-permute-start | bytes 1572872 | tf_op jit(solution)/shard_map/ppermute | solution.py:26
  134.0 57.5 %collective-permute-start.9 = (bf16[2,1,128,8,128]{2,4,3,1,0:T(8,128)(2,1)}, bf16[2,1,128,8,128]{2,4,3,1,0:T(8,128)(2,1)S(1)}, u32[]{:S(2)}, u32[]{:S(2)}) collective-permute-start(bf16[2,1,128,8,128]{2,4,3,1,0:T(8,128)(2,1)} %pad_maximum_fusion.4), channel_id=1, source_target_pairs={{32,0},{36,4},{40,8},{44,12},{48,16},{52,20},{56,24},{60,28},{64,3... | collective-permute-start | bytes 1572872 | tf_op jit(solution)/shard_map/ppermute | solution.py:26
  136.8 95.3 %collective-permute-start.10 = (bf16[2,1,128,8,128]{2,4,3,1,0:T(8,128)(2,1)}, bf16[2,1,128,8,128]{2,4,3,1,0:T(8,128)(2,1)S(1)}, u32[]{:S(2)}, u32[]{:S(2)}) collective-permute-start(bf16[2,1,128,8,128]{2,4,3,1,0:T(8,128)(2,1)} %pad_maximum_fusion.5), channel_id=1, source_target_pairs={{64,0},{68,4},{72,8},{76,12},{80,16},{84,20},{88,24},{92,28},{96,3... | collective-permute-start | bytes 1572872 | tf_op jit(solution)/shard_map/ppermute | solution.py:26
  140.2 91.9 %collective-permute-start.11 = (bf16[2,1,128,8,128]{2,4,3,1,0:T(8,128)(2,1)}, bf16[2,1,128,8,128]{2,4,3,1,0:T(8,128)(2,1)}, u32[]{:S(2)}, u32[]{:S(2)}) collective-permute-start(bf16[2,1,128,8,128]{2,4,3,1,0:T(8,128)(2,1)} %pad_maximum_fusion.6), channel_id=1, source_target_pairs={{128,0},{132,4},{136,8},{140,12},{144,16},{148,20},{152,24},{156,2... | collective-permute-start | bytes 1572872 | tf_op jit(solution)/shard_map/ppermute | solution.py:26
